TPU v7x, 32 devices: a whole 2x2x4 slice. The times are simulated.
32 devices in a mesh: row: 8 (over z, x), col: 4 (over y, core).
Axes of the slice: x: 2, y: 2, z: 4, core: 2. Of those that a mesh axis runs over, the one named last changes fastest.
Arguments:
- points: float32 [4096, 256], P('row'), may hold values from -6 to 6
- nugget: float32 [4096], P('row'), may hold values from 0.5 to 2
- weights: float32 [256], replicated, may hold values from 0.0005 to 0.005
- band_start: int32 [8], replicated, may hold values from 0 to 6, as said below
Outputs:
- factored: float32 [8, 2, 4, 512, 512], P('row', None, 'col')
Inputs may be any that keep to these rules, and one draw needn't show every extreme that they name: band_start[i] <= i - 1 for every i >= 1, band_start[0] = 0; band_start[5] = 0; the last tile row has band_start = 6.
All inputs are finite; a program needn't handle non-finite values.
Results may differ from a plain program's by a relative error of at most 0.0003.
Values sent between devices are 32-bit elements; how exact they have to be, the bound alone decides.
A program may use at most 128 MiB of HBM per device.

v0:
```python
import jax
import jax.numpy as jnp
from jax import lax
from jax.sharding import PartitionSpec as P


def broadcast(value, axis, source):
    kept = jnp.where(lax.axis_index(axis) == source, value, 0).astype(value.dtype)
    return lax.psum(kept, axis)


def kernel_tile(xrow, xcol, weights):
    weighted = xrow * weights
    sq_row = jnp.sum(weighted * xrow, axis=1)
    sq_col = jnp.sum(xcol * xcol * weights, axis=1)
    cross = jnp.dot(
        weighted, xcol.T, precision=lax.Precision.HIGHEST, preferred_element_type=jnp.float32
    )
    dist_sq = jnp.maximum(sq_row[:, None] + sq_col[None, :] - 2.0 * cross, 0.0)
    dist = jnp.sqrt(3.0 * dist_sq)
    return (1.0 + dist) * jnp.exp(-dist)


def factor_panel(local, p, n_col, my_row):
    owner_col = p % n_col
    diag_tile = broadcast(local, "row", p)
    lpp = jnp.linalg.cholesky(diag_tile)
    solved = jax.scipy.linalg.solve_triangular(lpp, local.T, lower=True).T
    panel = broadcast(solved, "col", owner_col)
    panel = jnp.where(my_row > p, panel, jnp.where(my_row == p, lpp, jnp.float32(0.0)))
    return panel


def column_factors(panel, my_col, n_col, blocks):
    width = panel.shape[1]
    slab = panel.shape[0] // (n_col * blocks)
    mixed = lax.all_to_all(panel, "row", split_axis=0, concat_axis=0, tiled=True)
    picked = lax.dynamic_slice_in_dim(mixed.reshape(blocks, n_col, slab, width), my_col, 1, 1)
    picked = picked.reshape(blocks, slab, width)
    whole = lax.all_gather(picked, "row", axis=1, tiled=True)
    return [whole[k] for k in range(blocks)]


def apply_panel(tiles, panel, col_tiles, p, my_row, my_col, n_col):
    result = []
    for k in range(len(tiles)):
        column = my_col + n_col * k
        prod = jnp.dot(
            panel,
            col_tiles[k].T,
            precision=lax.Precision.HIGHEST,
            preferred_element_type=jnp.float32,
        )
        live = (column > p) & (column <= my_row)
        block = tiles[k] - jnp.where(live, prod, jnp.float32(0.0))
        result.append(jnp.where(column == p, panel, block))
    return result


def body(points, nugget, weights, band_start):
    n_row = lax.axis_size("row")
    n_col = lax.axis_size("col")
    blocks = n_row // n_col
    my_row = lax.axis_index("row")
    my_col = lax.axis_index("col")
    diag_nugget = jnp.diag(nugget)
    tiles = []
    for k in range(blocks):
        column = my_col + n_col * k
        xcol = broadcast(points, "row", column)
        block = kernel_tile(points, xcol, weights)
        keep = (column >= band_start[my_row]) & (column <= my_row)
        block = jnp.where(keep, block, jnp.float32(0.0))
        tiles.append(block + jnp.where(column == my_row, diag_nugget, jnp.float32(0.0)))
    for p in range(2):
        panel = factor_panel(tiles[p // n_col], p, n_col, my_row)
        col_tiles = column_factors(panel, my_col, n_col, blocks)
        tiles = apply_panel(tiles, panel, col_tiles, p, my_row, my_col, n_col)
    stacked_tiles = jnp.stack(tiles)
    return stacked_tiles.reshape(1, blocks, 1, points.shape[0], points.shape[0])


def solution(mesh):
    placed = (P("row", None), P("row"), P(), P())
    return jax.shard_map(
        body,
        mesh=mesh,
        in_specs=placed,
        out_specs=P("row", None, "col", None, None),
        check_vma=False,
    )
```

profile of v0, /device:TPU:28, one launch (start us, length us, event | category | flops | bytes accessed | tf_op | source)
XLA Modules:
  0.0 822.8 jit_solution(575941400791107248)
XLA Ops:
  10.2 78.7 %all-reduce.16.cloned.1.call-done = (f32[512,256]{1,0:T(8,128)}, f32[512,256]{1,0:T(8,128)}) async-done(((f32[512,256]{1,0:T(8,128)}, f32[512,256]{1,0:T(8,128)}), (f32[512,256]{1,0:T(8,128)}, f32[512,256]{1,0:T(8,128)})) %all-reduce.16.cloned.1.call-update) | async-done | bytes 1048592 | tf_op jit(solution)/shard_map/psum | solution.py:9
  90.4 3.6 multiply_select_fusion
  97.9 77.5 %all-reduce.8.cloned.1.call-done = f32[512,512]{0,1:T(8,128)} async-done(((f32[512,512]{0,1:T(8,128)}), f32[512,512]{0,1:T(8,128)}) %all-reduce.8.cloned.1.call-update) | async-done | bytes 1048592 | tf_op jit(solution)/shard_map/psum | solution.py:9
  178.3 11.7 %cholesky.286 = f32[128,128]{1,0:T(8,128)S(1)} custom-call(f32[128,128]{1,0:T(8,128)S(1)} %cholesky.426), custom_call_target="Cholesky" | custom-call | tf_op jit(solution)/shard_map/jit(cholesky)/cholesky | solution.py:27
  190.2 9.8 %custom-call.27 = f32[1,128,128]{1,2,0:T(8,128)S(1)} custom-call(f32[1,128,128]{2,1,0:T(8,128)S(1)} %get-tuple-element.77), custom_call_target="InvertDiagBlocksLowerTriangular" | custom-call | tf_op jit(solution)/shard_map/jit(cholesky)/cholesky | solution.py:27
  202.7 11.7 %cholesky.305 = f32[128,128]{1,0:T(8,128)S(1)} custom-call(f32[128,128]{1,0:T(8,128)S(1)} %cholesky.430), custom_call_target="Cholesky" | custom-call | tf_op jit(solution)/shard_map/jit(cholesky)/cholesky | solution.py:27
  214.5 10.0 %custom-call.28 = f32[1,128,128]{1,2,0:T(8,128)S(1)} custom-call(f32[1,128,128]{2,1,0:T(8,128)S(1)} %get-tuple-element.75), custom_call_target="InvertDiagBlocksLowerTriangular" | custom-call | tf_op jit(solution)/shard_map/jit(cholesky)/cholesky | solution.py:27
  226.5 11.7 %cholesky.326 = f32[128,128]{1,0:T(8,128)S(1)} custom-call(f32[128,128]{1,0:T(8,128)S(1)} %cholesky.435), custom_call_target="Cholesky" | custom-call | tf_op jit(solution)/shard_map/jit(cholesky)/cholesky | solution.py:27
  238.4 9.8 %custom-call.29 = f32[1,128,128]{1,2,0:T(8,128)S(1)} custom-call(f32[1,128,128]{2,1,0:T(8,128)S(1)} %get-tuple-element.73), custom_call_target="InvertDiagBlocksLowerTriangular" | custom-call | tf_op jit(solution)/shard_map/jit(cholesky)/cholesky | solution.py:27
  249.8 12.1 %cholesky.343 = f32[128,128]{1,0:T(8,128)S(1)} custom-call(f32[128,128]{1,0:T(8,128)S(1)} %convolution_subtract_fusion.11), custom_call_target="Cholesky" | custom-call | tf_op jit(solution)/shard_map/jit(cholesky)/cholesky | solution.py:27
  267.7 12.2 %while.4 = (s32[]{:T(128)}, f32[512,512]{0,1:T(8,128)}, s32[4,2]{0,1:T(2,128)S(1)}, f32[4,128,128]{2,1,0:T(8,128)S(1)}, s32[]{:T(128)}) while((s32[]{:T(128)}, f32[512,512]{0,1:T(8,128)}, s32[4,2]{0,1:T(2,128)S(1)}, f32[4,128,128]{2,1,0:T(8,128)S(1)}, s32[]{:T(128)}) %tuple.53), condition=%wide.while_cond, body=%wide.while_body.sunk | while | flops 2 | bytes 393329 | solution.py:28
  279.9 39.3 %custom-call.30 = f32[4,128,128]{1,2,0:T(8,128)S(1)} custom-call(f32[4,128,128]{2,1,0:T(8,128)S(1)} %get-tuple-element.21), custom_call_target="InvertDiagBlocksLowerTriangular" | custom-call | tf_op jit(solution)/shard_map/jit(_solve_triangular)/triangular_solve | solution.py:28
  329.2 36.4 %all-reduce.10.cloned.1.call-done = f32[512,512]{0,1:T(8,128)} async-done(((f32[512,512]{0,1:T(8,128)}), f32[512,512]{0,1:T(8,128)}) %all-reduce.10.cloned.1.call-update) | async-done | bytes 1048592 | tf_op jit(solution)/shard_map/psum | solution.py:9
  368.3 6.0 all-to-all-start
  374.3 22.9 %all-to-all-done = f32[8,64,512]{2,1,0:T(8,128)S(1)} async-done(((f32[8,64,512]{2,1,0:T(8,128)}), f32[8,64,512]{2,1,0:T(8,128)S(1)}, u32[]{:S(2)}, u32[]{:S(2)}) %all-to-all-start) | async-done | bytes 1048608 | tf_op jit(solution)/shard_map/all_to_all | solution.py:37
  398.0 49.0 %all-gather.5.cloned.1.call-done = f32[2,1,512,512]{3,2,1,0:T(8,128)} async-done(((f32[2,1,64,512]{3,2,1,0:T(8,128)}), f32[2,1,512,512]{3,2,1,0:T(8,128)}) %all-gather.5.cloned.1.call-update) | async-done | bytes 2097168 | tf_op jit(solution)/shard_map/all_gather | solution.py:40
  447.1 4.1 broadcast_select_fusion
  451.4 76.8 %all-reduce.12.cloned.1.call-done = f32[512,512]{0,1:T(8,128)} async-done(((f32[512,512]{0,1:T(8,128)}), f32[512,512]{0,1:T(8,128)}) %all-reduce.12.cloned.1.call-update) | async-done | bytes 1048592 | tf_op jit(solution)/shard_map/psum | solution.py:9
  533.3 11.7 %cholesky.358 = f32[128,128]{1,0:T(8,128)S(1)} custom-call(f32[128,128]{1,0:T(8,128)S(1)} %cholesky.439), custom_call_target="Cholesky" | custom-call | tf_op jit(solution)/shard_map/jit(cholesky)/cholesky | solution.py:27
  546.4 9.8 %custom-call.31 = f32[1,128,128]{1,2,0:T(8,128)S(1)} custom-call(f32[1,128,128]{2,1,0:T(8,128)S(1)} %get-tuple-element.71), custom_call_target="InvertDiagBlocksLowerTriangular" | custom-call | tf_op jit(solution)/shard_map/jit(cholesky)/cholesky | solution.py:27
  558.8 11.7 %cholesky.377 = f32[128,128]{1,0:T(8,128)S(1)} custom-call(f32[128,128]{1,0:T(8,128)S(1)} %cholesky.443), custom_call_target="Cholesky" | custom-call | tf_op jit(solution)/shard_map/jit(cholesky)/cholesky | solution.py:27
  571.8 10.6 %custom-call.32 = f32[1,128,128]{1,2,0:T(8,128)} custom-call(f32[1,128,128]{2,1,0:T(8,128)S(1)} %get-tuple-element.69), custom_call_target="InvertDiagBlocksLowerTriangular" | custom-call | tf_op jit(solution)/shard_map/jit(cholesky)/cholesky | solution.py:27
  586.9 11.7 %cholesky.398 = f32[128,128]{1,0:T(8,128)S(1)} custom-call(f32[128,128]{1,0:T(8,128)S(1)} %cholesky.448), custom_call_target="Cholesky" | custom-call | tf_op jit(solution)/shard_map/jit(cholesky)/cholesky | solution.py:27
  598.8 9.8 %custom-call.33 = f32[1,128,128]{1,2,0:T(8,128)S(1)} custom-call(f32[1,128,128]{2,1,0:T(8,128)S(1)} %get-tuple-element.67), custom_call_target="InvertDiagBlocksLowerTriangular" | custom-call | tf_op jit(solution)/shard_map/jit(cholesky)/cholesky | solution.py:27
  610.2 12.1 %cholesky.415 = f32[128,128]{1,0:T(8,128)S(1)} custom-call(f32[128,128]{1,0:T(8,128)S(1)} %convolution_subtract_fusion.10), custom_call_target="Cholesky" | custom-call | tf_op jit(solution)/shard_map/jit(cholesky)/cholesky | solution.py:27
  629.9 12.4 %while.5 = (s32[]{:T(128)}, f32[512,512]{0,1:T(8,128)}, s32[4,2]{0,1:T(2,128)S(1)}, f32[4,128,128]{2,1,0:T(8,128)S(1)}, s32[]{:T(128)}) while((s32[]{:T(128)}, f32[512,512]{0,1:T(8,128)}, s32[4,2]{0,1:T(2,128)S(1)}, f32[4,128,128]{2,1,0:T(8,128)S(1)}, s32[]{:T(128)}) %tuple.74), condition=%wide.while_cond.clone, body=%wide.while_body.clone.sunk | while | flops 2 | bytes 393329 | solution.py:28
  643.0 40.1 %custom-call.34 = f32[4,128,128]{1,2,0:T(8,128)S(1)} custom-call(f32[4,128,128]{2,1,0:T(8,128)} %copy-done.11), custom_call_target="InvertDiagBlocksLowerTriangular" | custom-call | tf_op jit(solution)/shard_map/jit(_solve_triangular)/triangular_solve | solution.py:28
  690.3 36.4 %all-reduce.14.cloned.1.call-done = f32[512,512]{0,1:T(8,128)} async-done(((f32[512,512]{0,1:T(8,128)}), f32[512,512]{0,1:T(8,128)}) %all-reduce.14.cloned.1.call-update) | async-done | bytes 1048592 | tf_op jit(solution)/shard_map/psum | solution.py:9
  729.4 29.1 %all_to_all.18 = f32[8,64,512]{2,1,0:T(8,128)S(1)} all-to-all(f32[8,64,512]{2,1,0:T(8,128)} %bitcast.142), channel_id=1, replica_groups=mesh['row'=8,'col'=4] {'row'}, dimensions={0} | all-to-all | bytes 2097152 | tf_op jit(solution)/shard_map/all_to_all | solution.py:37
  764.7 4.9 fusion.6
  769.6 38.8 %all-gather.7.cloned.1.call-done = f32[2,1,512,512]{3,2,1,0:T(8,128)} async-done(((f32[2,1,64,512]{3,2,1,0:T(8,128)}), f32[2,1,512,512]{3,2,1,0:T(8,128)}) %all-gather.7.cloned.1.call-update) | async-done | bytes 2097168 | tf_op jit(solution)/shard_map/all_gather | solution.py:40
  808.4 3.3 fusion.9
  (181 shorter events, 100.3 us)
Async XLA Ops:
  6.5 82.4 %copy-start.2 = (f32[512,256]{1,0:T(8,128)S(1)}, f32[512,256]{1,0:T(8,128)}, u32[]{:S(2)}) copy-start(f32[512,256]{1,0:T(8,128)} %param.7) | copy-start | bytes 1572868
  6.5 2.3 copy-start.15
  6.5 82.4 %copy-start.13 = (f32[256]{0:T(256)S(1)}, f32[256]{0:T(256)}, u32[]{:S(2)}) copy-start(f32[256]{0:T(256)} %param.9) | copy-start | bytes 3076
  6.5 82.4 %all-reduce.16.cloned.1.call-start = ((), (), s32[]{:S(2)}) async-start(), calls=%async_computation.8 | async-start | bytes 2097152 | tf_op jit(solution)/shard_map/psum | solution.py:9
  8.7 166.7 %all-reduce.8.cloned.1.call-start = ((), (), s32[]{:S(2)}) async-start(), calls=%async_computation.2 | async-start | bytes 2097152 | tf_op jit(solution)/shard_map/psum | solution.py:9
  90.4 5.2 copy-start.12
  97.7 267.9 %all-reduce.10.cloned.1.call-start = ((), (), s32[]{:S(2)}) async-start(), calls=%async_computation.3 | async-start | bytes 2097152 | tf_op jit(solution)/shard_map/psum | solution.py:9
  175.5 1.7 copy-start.4
  177.3 1.0 copy-start.6
  368.3 28.9 %all-to-all-start = ((f32[8,64,512]{2,1,0:T(8,128)}), f32[8,64,512]{2,1,0:T(8,128)S(1)}, u32[]{:S(2)}, u32[]{:S(2)}) async-start(f32[8,64,512]{2,1,0:T(8,128)} %bitcast.14), calls=%async_computation | async-start | bytes 2097152 | tf_op jit(solution)/shard_map/all_to_all | solution.py:37
  374.3 72.8 %all-gather.5.cloned.1.call-start = ((), (), s32[]{:S(2)}) async-start(), calls=%async_computation.6 | async-start | bytes 2359296 | tf_op jit(solution)/shard_map/all_gather | solution.py:40
  398.0 130.3 %all-reduce.12.cloned.1.call-start = ((), (), s32[]{:S(2)}) async-start(), calls=%async_computation.4 | async-start | bytes 2097152 | tf_op jit(solution)/shard_map/psum | solution.py:9
  451.2 235.9 %copy-start = (f32[512,512]{0,1:T(8,128)}, f32[512,512]{0,1:T(8,128)S(1)}, u32[]{:S(2)}) copy-start(f32[512,512]{0,1:T(8,128)S(1)} %get-tuple-element.83) | copy-start | bytes 3145732
  451.2 275.4 %all-reduce.14.cloned.1.call-start = ((), (), s32[]{:S(2)}) async-start(), calls=%async_computation.5 | async-start | bytes 2097152 | tf_op jit(solution)/shard_map/psum | solution.py:9
  528.3 2.6 copy-start.5
  532.3 1.0 copy-start.7
  642.3 0.7 copy-start.11
  690.2 118.1 %all-gather.7.cloned.1.call-start = ((), (), s32[]{:S(2)}) async-start(), calls=%async_computation.7 | async-start | bytes 2359296 | tf_op jit(solution)/shard_map/all_gather | solution.py:40
  728.1 31.9 %copy-start.3 = (f32[512,256]{1,0:T(8,128)S(1)}, f32[512,256]{1,0:T(8,128)}, u32[]{:S(2)}) copy-start(f32[512,256]{1,0:T(8,128)} %param.7) | copy-start | bytes 1572868
  728.1 31.9 %copy-start.9 = (f32[512,256]{1,0:T(8,128)S(1)}, f32[512,256]{1,0:T(8,128)}, u32[]{:S(2)}) copy-start(f32[512,256]{1,0:T(8,128)} %get-tuple-element.59) | copy-start | bytes 1572868
  728.1 31.9 %copy-start.14 = (f32[256]{0:T(256)S(1)}, f32[256]{0:T(256)}, u32[]{:S(2)}) copy-start(f32[256]{0:T(256)} %param.9) | copy-start | bytes 3076
  764.7 43.7 %copy-start.1 = (f32[512,512]{0,1:T(8,128)S(1)}, f32[512,512]{0,1:T(8,128)}, u32[]{:S(2)}) copy-start(f32[512,512]{0,1:T(8,128)} %copy-done) | copy-start | bytes 3145732
  769.6 42.1 %copy-start.10 = (f32[512,512]{0,1:T(8,128)S(1)}, f32[512,512]{0,1:T(8,128)}, u32[]{:S(2)}) copy-start(f32[512,512]{0,1:T(8,128)} %fusion.6) | copy-start | bytes 3145732
  808.4 3.4 copy-start.8
Sparse Core Ops, SparseCore 0:
  10.9 77.9 all-reduce.15
  97.8 77.6 all-reduce.7
  329.3 36.2 all-reduce.9
  398.1 48.9 all-gather.4
  451.3 76.8 all-reduce.11
  690.4 36.2 all-reduce.13
  759.4 48.9 all-gather.6
where the time goes:
time: 830 us; the launch traced here: 823 us
  waiting for transfers between devices  417 us (50%)
  other arithmetic  256 us (31%)
  matrix products  47.5 us (6%)
  local copies, waits for them, and re-layouts  46.2 us (6%)
  blocking collectives  29.1 us (4%)
  between operations  20.8 us (3%)
    psum x5, waiting for transfers between devices, broadcast(): return lax.psum(kept, axis)  306 us
    another operation x29, other arithmetic, factor_panel(): lpp = jnp.linalg.cholesky(diag_tile)  161 us
    all_gather x2, waiting for transfers between devices, column_factors(): whole = lax.all_gather(picked, 'row', axis=1, tiled=True)  87.8 us
    another operation x5, other arithmetic, factor_panel(): solved = jax.scipy.linalg.solve_triangular(lpp, local.T, lower=True).T  81.6 us
    all_to_all x1, blocking collectives, column_factors(): lax.all_to_all(panel, 'row', split_axis=0, concat_axis=0, tiled=True)  29.1 us
    another operation x43, local copies, waits for them, and re-layouts, factor_panel(): solved = jax.scipy.linalg.solve_triangular(lpp, local.T, lower=True).T  24.3 us
    all_to_all x1, waiting for transfers between devices, column_factors(): lax.all_to_all(panel, 'row', split_axis=0, concat_axis=0, tiled=True)  22.9 us
  transfers between devices with their start and end apart: 8, of which 8 were waited for; matrix products, arithmetic and copies ran while one was open for 1% of the time, Pallas kernels for 0%

commit v1 on v0

v1 whole, which is shorter than its diff:
```python
import functools

import jax
import jax.numpy as jnp
from jax import lax
from jax.experimental import pallas as pl
from jax.experimental.pallas import tpu as pltpu
from jax.sharding import PartitionSpec as P

F32 = jnp.float32
BF16 = jnp.bfloat16
NB = 128
GROUP = 4
NT_DIMS = (((1,), (1,)), ((), ()))
TN_DIMS = (((0,), (0,)), ((), ()))
NN_DIMS = (((1,), (0,)), ((), ()))


def split(x):
    hi = x.astype(BF16)
    return hi, (x - hi.astype(F32)).astype(BF16)


def dot3(a, b, dims):
    def one(x, y):
        return lax.dot_general(x, y, dims, preferred_element_type=F32)

    return one(a[0], b[0]) + (one(a[0], b[1]) + one(a[1], b[0]))


def wide(x):
    return jnp.broadcast_to(x, (8, NB))


def invert_factor(aug, w_ref, k):
    n_slab = NB // 8
    at = pl.multiple_of(k * NB, NB)
    block = aug[pl.ds(at, NB), pl.ds(at, NB)]
    lane = lax.broadcasted_iota(jnp.int32, (8, NB), 1)
    sub = lax.broadcasted_iota(jnp.int32, (8, NB), 0)
    s = [block[8 * t : 8 * t + 8, :] for t in range(n_slab)]
    v = [jnp.where(lane == sub + 8 * t, 1.0, 0.0).astype(F32) for t in range(n_slab)]
    for j in range(0, NB, GROUP):
        first = j // 8
        rows = [wide(s[first][j % 8 + g : j % 8 + g + 1, :]) for g in range(GROUP)]
        vrows = [wide(v[first][j % 8 + g : j % 8 + g + 1, :]) for g in range(GROUP)]
        last = (j + GROUP) // 8
        cols = [
            {t: wide(s[t][:, j + g : j + g + 1]) for t in range(last, n_slab)}
            for g in range(GROUP)
        ]
        piv = [
            {h: wide(rows[g][:, j + h : j + h + 1]) for h in range(g, GROUP)}
            for g in range(GROUP)
        ]
        for g in range(GROUP):
            root = lax.rsqrt(piv[g][g])
            inv = root * root
            w_ref[j + g : j + g + 1, :] = (vrows[g] * root)[0:1, :]
            for h in range(g + 1, GROUP):
                f = piv[g][h] * inv
                for m in range(h, GROUP):
                    piv[h][m] = piv[h][m] - f * piv[g][m]
                rows[h] = rows[h] - f * rows[g]
                vrows[h] = vrows[h] - f * vrows[g]
                for t in cols[h]:
                    cols[h][t] = cols[h][t] - f * cols[g][t]
            q = rows[g] * inv
            vq = vrows[g] * inv
            for t in cols[g]:
                s[t] = s[t] - cols[g][t] * q
                v[t] = v[t] - cols[g][t] * vq


def factor(aug, u_ref, wh, wl, wk):
    size = aug.shape[0]
    n_block = size // NB
    row = lax.broadcasted_iota(jnp.int32, (size, size), 0)
    col = lax.broadcasted_iota(jnp.int32, (size, size), 1)
    aug[:, size:] = jnp.where(row == col, 1.0, 0.0).astype(F32)

    @pl.loop(0, n_block)
    def _(k):
        invert_factor(aug, wk, k)
        winv = split(wk[...])
        for kk in range(n_block):

            @pl.when(k == kk)
            def _():
                lo, hi = kk * NB, size + (kk + 1) * NB
                strip = dot3(winv, split(aug[lo : lo + NB, lo:hi]), NN_DIMS)
                parts = split(strip)
                u_ref[lo : lo + NB, lo:] = strip[:, : size - lo]
                wh[lo : lo + NB, : lo + NB] = parts[0][:, size - lo :]
                wl[lo : lo + NB, : lo + NB] = parts[1][:, size - lo :]
                if lo + NB < size:
                    zero = jnp.zeros((NB, size - lo - NB), BF16)
                    wh[lo : lo + NB, lo + NB :] = zero
                    wl[lo : lo + NB, lo + NB :] = zero
                    left = tuple(x[:, NB : size - lo] for x in parts)
                    right = tuple(x[:, NB:] for x in parts)
                    aug[lo + NB :, lo + NB : hi] -= dot3(left, right, TN_DIMS)


def prepare(y, slot, yh, yl, scol, srow):
    hi, lo = split(y)
    yh[slot], yl[slot] = hi, lo
    sq = y * y
    scol[slot] = jnp.sum(sq, axis=1, keepdims=True)
    srow[slot] = lax.dot_general(
        jnp.ones((8, y.shape[1]), F32), sq, NT_DIMS,
        precision=lax.Precision.HIGHEST, preferred_element_type=F32,
    )


def compute(i, c, n_col, blocks, g_ref, root_ref, band_ref, out_ref,
            aug, u_ref, wh, wl, wk, p0h, p0l, p1h, p1l, yh, yl, scol, srow):
    size = aug.shape[0]
    cov = g_ref.shape[-1]
    tiles = [0, 1, i] + [c + n_col * k for k in range(blocks)]

    def kernel_at(a, b, ta, tb, nugget=False):
        cross = dot3((yh[a], yl[a]), (yh[b], yl[b]), NT_DIMS)
        dist_sq = jnp.maximum(scol[a] + srow[b][0:1, :] - 2.0 * cross, 0.0)
        dist = jnp.sqrt(3.0 * dist_sq)
        value = (1.0 + dist) * jnp.exp(-dist)
        keep = (tb >= band_ref[ta]) & (tb <= ta)
        value = jnp.where(keep, value, 0.0)
        if nugget:
            extra = jnp.concatenate(
                [g_ref[ta, size + r : size + r + 1, :] for r in range(size // cov)], axis=1
            )
            row = lax.broadcasted_iota(jnp.int32, (size, size), 0)
            col = lax.broadcasted_iota(jnp.int32, (size, size), 1)
            value = value + jnp.where((row == col) & (ta == tb), extra, 0.0)
        return value

    for slot, t in enumerate(tiles):
        y = g_ref[t, :size, :] * root_ref[...]
        prepare(y, slot, yh, yl, scol, srow)

    def solved(a, hi_ref, lo_ref, slot):
        value = dot3(split(a), (wh[...], wl[...]), NT_DIMS)
        hi_ref[slot], lo_ref[slot] = split(value)
        return value

    def needed(slot, least):
        t = tiles[slot]
        return (t >= least) & (t <= i)

    aug[:, :size] = kernel_at(0, 0, 0, 0, True)
    factor(aug, u_ref, wh, wl, wk)
    row = lax.broadcasted_iota(jnp.int32, (size, size), 0)
    col = lax.broadcasted_iota(jnp.int32, (size, size), 1)

    @pl.when((i == 0) & (c == 0))
    def _():
        out_ref[0] = jnp.where(row <= col, u_ref[...], 0.0).T

    first = solved(kernel_at(1, 0, 1, 0), p0h, p0l, 1)

    @pl.when((i == 1) & (c == 0))
    def _():
        out_ref[0] = first

    aug[:, :size] = kernel_at(1, 1, 1, 1, True) - dot3(
        (p0h[1], p0l[1]), (p0h[1], p0l[1]), NT_DIMS
    )
    for slot in range(2, len(tiles)):

        @pl.when(needed(slot, 2))
        def _():
            value = solved(kernel_at(slot, 0, tiles[slot], 0), p0h, p0l, slot)
            if slot == 2:

                @pl.when(c == 0)
                def _():
                    out_ref[0] = value

    factor(aug, u_ref, wh, wl, wk)

    @pl.when((i == 1) & (c == 1))
    def _():
        out_ref[0] = jnp.where(row <= col, u_ref[...], 0.0).T

    for slot in range(2, len(tiles)):

        @pl.when(needed(slot, 2))
        def _():
            base = kernel_at(slot, 1, tiles[slot], 1) - dot3(
                (p0h[slot], p0l[slot]), (p0h[1], p0l[1]), NT_DIMS
            )
            value = solved(base, p1h, p1l, slot)
            if slot == 2:

                @pl.when(c == 1)
                def _():
                    out_ref[0] = value

    for k in range(blocks):
        slot = 3 + k
        t = tiles[slot]

        @pl.when(needed(slot, 2))
        def _():
            value = kernel_at(2, slot, i, t, True)
            value = value - dot3((p0h[2], p0l[2]), (p0h[slot], p0l[slot]), NT_DIMS)
            out_ref[k] = value - dot3((p1h[2], p1l[2]), (p1h[slot], p1l[slot]), NT_DIMS)

        @pl.when(t > i)
        def _():
            out_ref[k] = jnp.zeros((size, size), F32)


def plain_kernel(n_col, blocks, where_ref, band_ref, g_ref, root_ref, out_ref, *scratch):
    compute(where_ref[0], where_ref[1], n_col, blocks, g_ref, root_ref, band_ref, out_ref, *scratch)


def scratch_list(size, cov, blocks):
    slots = 3 + blocks
    return [
        pltpu.VMEM((size, 2 * size), F32),
        pltpu.VMEM((size, size), F32),
        pltpu.VMEM((size, size), BF16),
        pltpu.VMEM((size, size), BF16),
        pltpu.VMEM((NB, NB), F32),
        pltpu.VMEM((slots, size, size), BF16),
        pltpu.VMEM((slots, size, size), BF16),
        pltpu.VMEM((slots, size, size), BF16),
        pltpu.VMEM((slots, size, size), BF16),
        pltpu.VMEM((slots, size, cov), BF16),
        pltpu.VMEM((slots, size, cov), BF16),
        pltpu.VMEM((slots, size, 1), F32),
        pltpu.VMEM((slots, 8, size), F32),
    ]


def run_plain(where, band, gathered, root, n_col, blocks, interpret=False):
    size, cov = gathered.shape[1] - 8, gathered.shape[2]
    smem = pl.BlockSpec(memory_space=pltpu.SMEM)
    vmem = pl.BlockSpec(memory_space=pltpu.VMEM)
    return pl.pallas_call(
        functools.partial(plain_kernel, n_col, blocks),
        out_shape=jax.ShapeDtypeStruct((blocks, size, size), F32),
        in_specs=[smem, smem, vmem, vmem],
        out_specs=vmem,
        scratch_shapes=scratch_list(size, cov, blocks),
        compiler_params=pltpu.CompilerParams(vmem_limit_bytes=58 * 1024 * 1024),
        interpret=interpret,
    )(where, band, gathered, root)


def body(points, nugget, weights, band_start):
    n_row = lax.axis_size("row")
    n_col = lax.axis_size("col")
    blocks = n_row // n_col
    size, cov = points.shape
    where = jnp.stack([lax.axis_index("row"), lax.axis_index("col")]).astype(jnp.int32)
    extra = nugget.reshape(size // cov, cov)
    packed = jnp.concatenate([points, extra, jnp.zeros((8 - size // cov, cov), F32)])
    gathered = lax.all_gather(packed, "row")
    tiles = run_plain(where, band_start, gathered, jnp.sqrt(weights)[None, :], n_col, blocks)
    return tiles.reshape(1, blocks, 1, size, size)


def solution(mesh):
    placed = (P("row", None), P("row"), P(), P())
    return jax.shard_map(
        body,
        mesh=mesh,
        in_specs=placed,
        out_specs=P("row", None, "col", None, None),
        check_vma=False,
    )
```

time: 830 us -> 171 us (0.21)
  waiting for transfers between devices: 417 us -> 71.8 us
  other arithmetic: 256 us -> 2.59 us
  Pallas kernels: 0 us -> 81 us
  matrix products: 47.5 us -> 0 us
  local copies, waits for them, and re-layouts: 46.2 us -> 2.03 us
  blocking collectives: 29.1 us -> 0 us
    psum x5 -> x0, waiting for transfers between devices: 306 us -> none  [broadcast(): return lax.psum(kept, axis)]
    another operation x34 -> x1, other arithmetic: 243 us -> 0.62 us  [body(): jnp.stack([lax.axis_index('row'), lax.axis_index('col')]).astype(jnp.int32)]
    pallas_call x0 -> x1, Pallas kernels: none -> 81 us  [run_plain(): pl.pallas_call(functools.partial(plain_kernel, n_col, blocks), out_shape=...]
    all_to_all x1 -> x0, blocking collectives: 29.1 us -> none  [column_factors(): lax.all_to_all(panel, 'row', split_axis=0, concat_axis=0, tiled=True)]
    another operation x69 -> x0, local copies, waits for them, and re-layouts: 28.6 us -> none  [the longest x43 24.3 us: factor_panel(): solved = jax.scipy.linalg.solve_triangular(lpp, local.T, lower=True).T]
    another operation x26 -> x0, matrix products: 27.4 us -> none  [the longest x14 14.7 us: factor_panel(): solved = jax.scipy.linalg.solve_triangular(lpp, local.T, lower=True).T]
    all_to_all x1 -> x0, waiting for transfers between devices: 22.9 us -> none  [column_factors(): lax.all_to_all(panel, 'row', split_axis=0, concat_axis=0, tiled=True)]
    dot_general x6 -> x0, matrix products: 20.1 us -> none  [the longest x4 14.4 us: apply_panel(): jnp.dot(panel, col_tiles[k].T, precision=lax.Precision.HIGHEST, preferred...]
  transfers between devices with their start and end apart: 8 -> 1, of which waited for: 8 -> 1; matrix products, arithmetic and copies ran while one was open for 1% -> 1% of each run, Pallas kernels for 0% -> 0%
where the time goes in v1:
time: 171 us
  Pallas kernels  81 us (47%)
  waiting for transfers between devices  71.8 us (42%)
  between operations  13.4 us (8%)
  other arithmetic  2.59 us (2%)
  local copies, waits for them, and re-layouts  2.03 us (1%)
    pallas_call x1, Pallas kernels, run_plain(): pl.pallas_call(functools.partial(plain_kernel, n_col, blocks), out_shape=...  81 us
    all_gather x1, waiting for transfers between devices, body(): gathered = lax.all_gather(packed, 'row')  71.7 us
  transfers between devices with their start and end apart: 1, of which 1 were waited for; matrix products, arithmetic and copies ran while one was open for 1% of the time, Pallas kernels for 0%

profile of v1, /device:TPU:28, one launch (start us, length us, event | category | flops | bytes accessed | tf_op | source)
XLA Modules:
  0.0 170.7 jit_solution(9860518540429801683)
XLA Ops:
  6.5 0.0 all-gather.3.cloned.1.call-start
  6.5 0.7 reshape.6
  7.2 0.1 pad.2.clone
  7.3 2.0 %maximum_maximum_fusion = f32[520,256]{1,0:T(8,128)} fusion(f32[2,256]{1,0:T(2,128)S(1)} %reshape.6, f32[512,256]{1,0:T(8,128)} %param.4, f32[520]{0:T(1024)S(1)} %pad.2.clone), kind=kLoop, calls=%fused_computation | loop fusion | flops 266240 | bytes 1060896 | tf_op jit(solution)/shard_map/concatenate | solution.py:260
  9.3 0.0 all-gather.3.cloned.1.call-update
  9.3 1.3 sqrt.3
  10.6 0.6 pad_add_fusion.where_ref
  11.2 71.7 %all-gather.3.cloned.1.call-done = f32[4160,256]{1,0:T(8,128)} async-done(((f32[520,256]{1,0:T(8,128)}), f32[4160,256]{1,0:T(8,128)}) %all-gather.3.cloned.1.call-update) | async-done | bytes 4259856 | tf_op jit(solution)/shard_map/all_gather | solution.py:261
  82.9 81.0 %shard_map.46 = f32[2,512,512]{2,1,0:T(8,128)} custom-call(s32[2]{0:T(128)} %pad_add_fusion.where_ref, s32[8]{0:T(128)} %band_ref.1, f32[8,520,256]{2,1,0:T(8,128)} %bitcast.7, f32[1,256]{1,0:T(1,128)} %bitcast.8), custom_call_target="tpu_custom_call" | custom-call | tf_op jit(solution)/shard_map/pallas_call | solution.py:242
  (1 shorter events, 0.0 us)
Async XLA Ops:
  6.5 76.4 %all-gather.3.cloned.1.call-start = ((), (), s32[]{:S(2)}) async-start(), calls=%async_computation | async-start | bytes 4792320 | tf_op jit(solution)/shard_map/all_gather | solution.py:261
Sparse Core Ops, SparseCore 0:
  9.5 73.3 all-gather.2

commit v2 on v1

--- a/solution.py
+++ b/solution.py
@@ -236,7 +236,7 @@
 
 
 def run_plain(where, band, gathered, root, n_col, blocks, interpret=False):
-    size, cov = gathered.shape[1] - 8, gathered.shape[2]
+    size, cov = gathered.shape[1] - 8 * n_col, gathered.shape[2]
     smem = pl.BlockSpec(memory_space=pltpu.SMEM)
     vmem = pl.BlockSpec(memory_space=pltpu.VMEM)
     return pl.pallas_call(
@@ -257,8 +257,12 @@
     size, cov = points.shape
     where = jnp.stack([lax.axis_index("row"), lax.axis_index("col")]).astype(jnp.int32)
     extra = nugget.reshape(size // cov, cov)
-    packed = jnp.concatenate([points, extra, jnp.zeros((8 - size // cov, cov), F32)])
-    gathered = lax.all_gather(packed, "row")
+    pad = 8 * n_col
+    packed = jnp.concatenate([points, extra, jnp.zeros((pad - size // cov, cov), F32)])
+    share = (size + pad) // n_col
+    mine = lax.dynamic_slice_in_dim(packed, lax.axis_index("col") * share, share)
+    gathered = lax.all_gather(mine, ("row", "col"), tiled=True)
+    gathered = gathered.reshape(n_row, size + pad, cov)
     tiles = run_plain(where, band_start, gathered, jnp.sqrt(weights)[None, :], n_col, blocks)
     return tiles.reshape(1, blocks, 1, size, size)
 

time: 171 us -> 161 us (0.942)
  waiting for transfers between devices: 71.8 us -> 61.7 us
    all_gather x1, waiting for transfers between devices: 71.7 us -> 61.7 us  [body(): gathered = lax.all_gather(mine, ('row', 'col'), tiled=True)]
where the time goes in v2:
time: 161 us; the launch traced here: 160 us
  Pallas kernels  81 us (50%)
  waiting for transfers between devices  61.7 us (38%)
  between operations  13.4 us (8%)
  other arithmetic  2.3 us (1%)
  local copies, waits for them, and re-layouts  2 us (1%)
    pallas_call x1, Pallas kernels, run_plain(): pl.pallas_call(functools.partial(plain_kernel, n_col, blocks), out_shape=...  81 us
    all_gather x1, waiting for transfers between devices, body(): gathered = lax.all_gather(mine, ('row', 'col'), tiled=True)  61.7 us
  transfers between devices with their start and end apart: 1, of which 1 were waited for; matrix products, arithmetic and copies ran while one was open for 1% of the time, Pallas kernels for 0%

profile of v2, /device:TPU:28, one launch (start us, length us, event | category | flops | bytes accessed | tf_op | source)
XLA Modules:
  0.0 160.4 jit_solution(2134585437310702453)
XLA Ops:
  6.5 0.0 all-gather.2.cloned.1.call-start
  6.5 0.7 reshape.9
  7.2 0.1 pad_dynamic-slice_fusion.2
  7.3 1.7 %fusion.1 = f32[136,256]{1,0:T(8,128)} fusion(s32[]{:T(128)S(6)} %select_n.3, f32[512,256]{1,0:T(8,128)} %param.4, f32[2,256]{1,0:T(2,128)S(1)} %reshape.9, f32[136]{0:T(256)S(1)} %pad_dynamic-slice_fusion.2), kind=kLoop, calls=%fused_computation.3 | loop fusion | flops 69632 | bytes 666148 | tf_op jit(solution)/shard_map/concatenate | solution.py:261
  9.0 0.0 all-gather.2.cloned.1.call-update
  9.0 1.2 sqrt.3
  10.2 0.7 pad_add_fusion.where_ref
  10.9 61.7 %all-gather.2.cloned.1.call-done = f32[4352,256]{1,0:T(8,128)} async-done(((f32[136,256]{1,0:T(8,128)}), f32[4352,256]{1,0:T(8,128)}) %all-gather.2.cloned.1.call-update) | async-done | bytes 4456464 | tf_op jit(solution)/shard_map/all_gather | solution.py:264
  72.5 81.0 %shard_map.46 = f32[2,512,512]{2,1,0:T(8,128)} custom-call(s32[2]{0:T(128)} %pad_add_fusion.where_ref, s32[8]{0:T(128)} %band_ref.1, f32[8,544,256]{2,1,0:T(8,128)} %bitcast.7, f32[1,256]{1,0:T(1,128)} %bitcast.8), custom_call_target="tpu_custom_call" | custom-call | tf_op jit(solution)/shard_map/pallas_call | solution.py:242
  (1 shorter events, 0.0 us)
Async XLA Ops:
  6.5 66.0 %all-gather.2.cloned.1.call-start = ((), (), s32[]{:S(2)}) async-start(), calls=%async_computation | async-start | bytes 4595712 | tf_op jit(solution)/shard_map/all_gather | solution.py:264
Sparse Core Ops, SparseCore 0:
  10.2 62.2 all-gather.1
